TPU v7x, 32 devices: a whole 2x2x4 slice. The times are simulated.
32 devices in a mesh: space: 16 (over z, x, core), snap: 2 (over y).
Axes of the slice: x: 2, y: 2, z: 4, core: 2. Of those that a mesh axis runs over, the one named last changes fastest.
Arguments:
- snapshots: bfloat16 [65536, 512], P('space', 'snap'), may hold values from -6 to 6
- basis: bfloat16 [65536, 64], P('space'), may hold values from -0.0234375 to 0.0234375
Outputs:
- normal: float32 [2144, 2144], P('snap')
- rhs: float32 [2144, 64], P('snap')
All inputs are finite; a program needn't handle non-finite values.
Results may differ from a plain program's by a relative error of at most 0.0034.
Values sent between devices are 32-bit elements; how exact they have to be, the bound alone decides.
A program may use at most 64 MiB of HBM per device.

v0:
```python
import jax
import jax.numpy as jnp
import numpy as np
from jax import lax
from jax.sharding import PartitionSpec as P


def row_block(states, diffs, total_snaps):
    rank = states.shape[0]
    upper_rows, upper_cols = np.triu_indices(rank)
    quad = states[upper_rows, :] * states[upper_cols, :]
    features = jnp.concatenate([states, quad], axis=0).T.astype(jnp.bfloat16)
    targets = diffs.T.astype(jnp.bfloat16)
    width = features.shape[1]
    block_rows = width // lax.axis_size("snap")
    chosen = lax.dynamic_slice_in_dim(features, lax.axis_index("snap") * block_rows, block_rows, 1)
    dims = (((0,), (0,)), ((), ()))
    normal = (
        lax.dot_general(chosen, features, dims, preferred_element_type=jnp.float32) / total_snaps
    )
    rhs = lax.dot_general(chosen, targets, dims, preferred_element_type=jnp.float32) / total_snaps
    return (normal, rhs)


def per_device(snapshots, basis):
    partial_value = lax.dot_general(
        basis, snapshots, (((0,), (0,)), ((), ())), preferred_element_type=jnp.float32
    )
    total_snaps = snapshots.shape[1] * lax.axis_size("snap")
    summed = lax.psum(partial_value, "space")
    states = lax.all_gather(summed, "snap", axis=1, tiled=True)
    diffs = jnp.roll(states, -1, axis=1) - states
    normal, rhs = row_block(states, diffs, total_snaps)
    return (normal, rhs)


def solution(mesh):
    return jax.shard_map(
        per_device,
        mesh=mesh,
        in_specs=(P("space", "snap"), P("space", None)),
        out_specs=(P("snap", None), P("snap", None)),
        check_vma=False,
    )
```

profile of v0, /device:TPU:0, one launch (start us, length us, event | category | flops | bytes accessed | tf_op | source)
XLA Modules:
  0.0 135.7 jit_solution(3106232466726738440)
XLA Ops:
  7.2 0.0 copy-start
  7.2 0.0 copy-start.3
  7.2 0.0 copy-start.4
  7.2 0.0 all-reduce.2.cloned.1.call-start
  7.2 1.5 %copy-done = bf16[4096,256]{1,0:T(8,128)(2,1)S(1)} copy-done((bf16[4096,256]{1,0:T(8,128)(2,1)S(1)}, bf16[4096,256]{1,0:T(8,128)(2,1)}, u32[]{:S(2)}) %copy-start) | copy-done | bytes 2097176
  8.8 2.1 %fusion.8 = f32[64,256]{1,0:T(8,128)} fusion(bf16[4096,64]{0,1:T(8,128)(2,1)} %param.7, bf16[4096,256]{1,0:T(8,128)(2,1)S(1)} %copy-done), kind=kOutput, calls=%fused_computation.16 | convolution fusion | flops 134217728 | bytes 2686976 | tf_op jit(solution)/shard_map/dot_general | solution.py:26
  10.9 0.0 all-reduce.2.cloned.1.call-update
  10.9 0.0 copy-done.3
  11.0 0.0 copy-done.4
  11.0 88.3 %all-reduce.2.cloned.1.call-done = f32[64,256]{1,0:T(8,128)} async-done(((f32[64,256]{1,0:T(8,128)}), f32[64,256]{1,0:T(8,128)}) %all-reduce.2.cloned.1.call-update) | async-done | bytes 65552 | tf_op jit(solution)/shard_map/psum | solution.py:30
  99.3 5.2 %all_gather.3 = f32[64,512]{1,0:T(8,128)S(1)} all-gather(f32[64,256]{1,0:T(8,128)} %all-reduce.2.cloned.1.call-done), channel_id=1, replica_groups=mesh['space'=16,'snap'=2] {'snap'}, dimensions={1}, use_global_device_ids=true | all-gather | bytes 196608 | tf_op jit(solution)/shard_map/all_gather | solution.py:31
  104.5 0.0 copy-start.1
  104.5 0.1 slice.14
  104.6 6.8 %gather_fusion.1 = f32[2080,512]{1,0:T(8,128)} fusion(f32[64,512]{1,0:T(8,128)S(1)} %all_gather.3, s32[3072]{0:T(1024)S(1)} %pad_clamp_fusion), kind=kCustom, calls=%fused_computation.1 | custom fusion | bytes 8528000 | tf_op jit(solution)/shard_map/gather | solution.py:11
  111.3 0.0 copy-done.1
  111.3 6.8 %gather_fusion = f32[2080,512]{1,0:T(8,128)} fusion(f32[64,512]{1,0:T(8,128)S(1)} %all_gather.3, s32[3072]{0:T(1024)S(1)} %pad_clamp_fusion.1), kind=kCustom, calls=%fused_computation | custom fusion | bytes 8528000 | tf_op jit(solution)/shard_map/gather | solution.py:11
  118.1 4.2 %multiply_convert_fusion = bf16[2080,512]{1,0:T(8,128)(2,1)S(1)} fusion(f32[2080,512]{1,0:T(8,128)} %gather_fusion, f32[2080,512]{1,0:T(8,128)} %gather_fusion.1), kind=kLoop, calls=%fused_computation.3 | loop fusion | flops 2129920 | bytes 10649600 | tf_op jit(solution)/shard_map/convert.1
  122.4 0.0 copy-start.2
  122.4 0.0 slice-start
  122.4 5.2 %convolution_multiply_fusion = f32[1072,2144]{1,0:T(8,128)} fusion(bf16[64,512]{1,0:T(8,128)(2,1)S(1)} %convert.6, bf16[2080,512]{1,0:T(8,128)(2,1)S(1)} %multiply_convert_fusion, s32[]{:T(128)S(6)} %select_n.11), kind=kOutput, calls=%fused_computation.2 | convolution fusion | flops 2362413568 | bytes 13584388 | tf_op jit(solution)/shard_map/dot_general | solution.py:19
  127.6 0.0 copy-done.2
  127.6 0.0 slice-done
  127.6 1.2 convolution_multiply_fusion.1
  (3 shorter events, 0.0 us)
Async XLA Ops:
  7.2 1.6 %copy-start = (bf16[4096,256]{1,0:T(8,128)(2,1)S(1)}, bf16[4096,256]{1,0:T(8,128)(2,1)}, u32[]{:S(2)}) copy-start(bf16[4096,256]{1,0:T(8,128)(2,1)} %param.6) | copy-start | bytes 6291460
  7.2 3.8 %copy-start.3 = (s32[2080]{0:T(1024)S(1)}, s32[2080]{0:T(1024)}, u32[]{:S(2)}) copy-start(s32[2080]{0:T(1024)} %constant.28) | copy-start | bytes 24964
  7.2 3.8 %copy-start.4 = (s32[2080]{0:T(1024)S(1)}, s32[2080]{0:T(1024)}, u32[]{:S(2)}) copy-start(s32[2080]{0:T(1024)} %constant.29) | copy-start | bytes 24964
  7.2 92.1 %all-reduce.2.cloned.1.call-start = ((), (), s32[]{:S(2)}) async-start(), calls=%async_computation | async-start | bytes 131072 | tf_op jit(solution)/shard_map/psum | solution.py:30
  104.5 6.9 %copy-start.1 = (f32[64,512]{1,0:T(8,128)}, f32[64,512]{1,0:T(8,128)S(1)}, u32[]{:S(2)}) copy-start(f32[64,512]{1,0:T(8,128)S(1)} %all_gather.3) | copy-start | bytes 393220
  122.4 5.3 %copy-start.2 = (f32[64,512]{1,0:T(8,128)S(1)}, f32[64,512]{1,0:T(8,128)}, u32[]{:S(2)}) copy-start(f32[64,512]{1,0:T(8,128)} %copy-done.1) | copy-start | bytes 393220
  122.4 5.3 %slice-start = ((f32[64,512]{1,0:T(8,128)}), f32[64,1]{1,0:T(8,128)S(1)}, s32[]{:S(2)}) async-start(f32[64,512]{1,0:T(8,128)} %copy-done.1), calls=%async_computation.1 | async-start | bytes 65536 | tf_op jit(solution)/shard_map/jit(_roll_static)/slice | solution.py:32
Sparse Core Ops, SparseCore 0:
  12.1 87.1 all-reduce.1
where the time goes:
time: 137 us; the launch traced here: 136 us
  waiting for transfers between devices  88.3 us (64%)
  local copies, waits for them, and re-layouts  15.2 us (11%)
  between operations  14.1 us (10%)
  matrix products  8.58 us (6%)
  blocking collectives  5.18 us (4%)
  other arithmetic  4.27 us (3%)
    psum x1, waiting for transfers between devices, per_device(): summed = lax.psum(partial_value, 'space')  88.3 us
    gather x2, local copies, waits for them, and re-layouts, row_block(): quad = states[upper_rows, :] * states[upper_cols, :]  13.5 us
    dot_general x1, matrix products, row_block(): lax.dot_general(chosen, features, dims, preferred_element_type=jnp.float32)  5.24 us
    all_gather x1, blocking collectives, per_device(): states = lax.all_gather(summed, 'snap', axis=1, tiled=True)  5.18 us
    another operation x2, other arithmetic  4.25 us
  transfers between devices with their start and end apart: 1, of which 1 were waited for; matrix products, arithmetic and copies ran while one was open for 0% of the time, Pallas kernels for 0%

commit v1 on v0

v1 whole, which is shorter than its diff:
```python
import functools

import jax
import jax.numpy as jnp
import numpy as np
from jax import lax
from jax.experimental import pallas as pl
from jax.experimental.pallas import tpu as pltpu
from jax.sharding import PartitionSpec as P

MESH = pl.DeviceIdType.MESH
SUB, LANE = 8, 128
LOADS = 4


def states_kernel(n, m, snaps_hbm, basis_hbm, out_ref, snaps, basis, part, recv, gath, load_sem, sems):
    me, grp = lax.axis_index("space"), lax.axis_index("snap")
    peers = [(dp, ds) for ds in range(m) for dp in range(n) if dp or ds]

    step = snaps.shape[0] // LOADS
    loads = []
    for k in range(LOADS):
        rows = pl.ds(k * step, step)
        loads.append(
            (
                pltpu.make_async_copy(snaps_hbm.at[rows], snaps.at[rows], load_sem.at[0, k]),
                pltpu.make_async_copy(basis_hbm.at[:, rows], basis.at[:, rows], load_sem.at[1, k]),
            )
        )
        for load in loads[-1]:
            load.start()

    def device(dp, ds):
        return (lax.rem(me + dp, n), lax.rem(grp + ds, m))

    barrier = pltpu.get_barrier_semaphore()
    for dp, ds in peers:
        pl.semaphore_signal(barrier, inc=1, device_id=device(dp, ds), device_id_type=MESH)

    total = None
    for k in range(LOADS):
        for load in loads[k]:
            load.wait()
        piece = jnp.dot(
            basis[:, k * step : (k + 1) * step],
            snaps[k * step : (k + 1) * step, :],
            preferred_element_type=jnp.float32,
        )
        total = piece if total is None else total + piece
    rank, width = total.shape
    wide = width // LANE
    for r in range(rank // SUB):
        for q in range(wide):
            part[r * wide + q] = total[r * SUB : (r + 1) * SUB, q * LANE : (q + 1) * LANE]

    pl.semaphore_wait(barrier, len(peers))

    for dp in range(1, n):
        to = device(dp, 0)
        pltpu.make_async_remote_copy(
            src_ref=part.at[to[0]],
            dst_ref=recv.at[dp - 1],
            send_sem=sems.at[0],
            recv_sem=sems.at[1],
            device_id=to,
            device_id_type=MESH,
        ).start()
    pltpu.make_async_copy(recv, recv, sems.at[1]).wait()
    tile = part[me]
    for dp in range(1, n):
        tile = tile + recv[dp - 1]
    slot = grp * n + me
    gath[slot] = tile

    for dp, ds in peers:
        pltpu.make_async_remote_copy(
            src_ref=gath.at[slot],
            dst_ref=gath.at[slot],
            send_sem=sems.at[2],
            recv_sem=sems.at[3],
            device_id=device(dp, ds),
            device_id_type=MESH,
        ).start()
    others = gath.at[pl.ds(0, len(peers))]
    pltpu.make_async_copy(others, others, sems.at[3]).wait()
    for s in range(m):
        for r in range(rank // SUB):
            for q in range(wide):
                out_ref[r * SUB : (r + 1) * SUB, s * width + q * LANE : s * width + (q + 1) * LANE] = (
                    gath[s * n + r * wide + q]
                )
    pltpu.make_async_copy(recv, recv, sems.at[0]).wait()
    pltpu.make_async_copy(others, others, sems.at[2]).wait()


def all_states(snapshots, basis):
    n, m = lax.axis_size("space"), lax.axis_size("snap")
    rows, width = snapshots.shape
    rank = basis.shape[1]
    if n * SUB * LANE != rank * width:
        partial_value = lax.dot_general(
            basis, snapshots, (((0,), (0,)), ((), ())), preferred_element_type=jnp.float32
        )
        return lax.all_gather(lax.psum(partial_value, "space"), "snap", axis=1, tiled=True)
    return pl.pallas_call(
        functools.partial(states_kernel, n, m),
        out_shape=jax.ShapeDtypeStruct((rank, width * m), jnp.float32),
        in_specs=[pl.BlockSpec(memory_space=pl.ANY)] * 2,
        out_specs=pl.BlockSpec(memory_space=pltpu.VMEM),
        scratch_shapes=[
            pltpu.VMEM((rows, width), jnp.bfloat16),
            pltpu.VMEM((rank, rows), jnp.bfloat16),
            pltpu.VMEM((n, SUB, LANE), jnp.float32),
            pltpu.VMEM((n - 1, SUB, LANE), jnp.float32),
            pltpu.VMEM((n * m, SUB, LANE), jnp.float32),
            pltpu.SemaphoreType.DMA((2, LOADS)),
            pltpu.SemaphoreType.DMA((4,)),
        ],
        compiler_params=pltpu.CompilerParams(
            collective_id=0, has_side_effects=True, vmem_limit_bytes=32 * 2**20
        ),
        name="states",
    )(snapshots, basis.T)


COLS = 256


def normal_kernel(m, states_ref, normal_hbm, rhs_ref, quad, feats, normal, sems):
    rank, snaps = states_ref.shape
    width = rank + rank * (rank + 1) // 2
    rows = width // m
    states = states_ref[...]

    for a in range(rank - 1, -1, -1):
        lead = a % SUB
        start = rank + a * rank - a * (a - 1) // 2
        quad[start - lead : start - a + rank, :] = states[a - lead :, :] * states[a : a + 1, :]
    quad[:rank, :] = states
    feats[...] = quad[...].astype(jnp.bfloat16)

    scale = 1.0 / snaps
    mine = pl.multiple_of(lax.axis_index("snap") * rows, 16)
    dims = (((1,), (1,)), ((), ()))
    copies = []
    for j in range(0, width, COLS):
        cols = min(COLS, width - j)
        normal[:, j : j + cols] = (
            lax.dot_general(
                feats[pl.ds(mine, rows), :],
                feats[j : j + cols, :],
                dims,
                preferred_element_type=jnp.float32,
            )
            * scale
        )
        copies.append(
            pltpu.make_async_copy(
                normal.at[:, j : j + cols], normal_hbm.at[:, j : j + cols], sems.at[j // COLS]
            )
        )
        copies[-1].start()
    ahead = jnp.concatenate([states[:, 1:], states[:, :1]], axis=1)
    targets = (ahead - states).astype(jnp.bfloat16)
    rhs_ref[...] = (
        lax.dot_general(
            targets, feats[pl.ds(mine, rows), :], dims, preferred_element_type=jnp.float32
        )
        * scale
    )
    for copy in copies:
        copy.wait()


def row_block(states):
    rank, snaps = states.shape
    m = lax.axis_size("snap")
    width = rank + rank * (rank + 1) // 2
    rows = width // m
    if rows % 16 == 0:
        normal, rhs = pl.pallas_call(
            functools.partial(normal_kernel, m),
            out_shape=(
                jax.ShapeDtypeStruct((rows, width), jnp.float32),
                jax.ShapeDtypeStruct((rank, rows), jnp.float32),
            ),
            in_specs=[pl.BlockSpec(memory_space=pltpu.VMEM)],
            out_specs=(
                pl.BlockSpec(memory_space=pl.ANY),
                pl.BlockSpec(memory_space=pltpu.VMEM),
            ),
            scratch_shapes=[
                pltpu.VMEM((width, snaps), jnp.float32),
                pltpu.VMEM((width, snaps), jnp.bfloat16),
                pltpu.VMEM((rows, width), jnp.float32),
                pltpu.SemaphoreType.DMA((-(-width // COLS),)),
            ],
            compiler_params=pltpu.CompilerParams(vmem_limit_bytes=40 * 2**20),
            name="normal",
        )(states)
        return normal, rhs.T
    upper_rows, upper_cols = np.triu_indices(rank)
    quad = states[upper_rows, :] * states[upper_cols, :]
    features = jnp.concatenate([states, quad], axis=0).T.astype(jnp.bfloat16)
    targets = (jnp.roll(states, -1, axis=1) - states).T.astype(jnp.bfloat16)
    chosen = lax.dynamic_slice_in_dim(features, lax.axis_index("snap") * rows, rows, 1)
    dims = (((0,), (0,)), ((), ()))
    normal = lax.dot_general(chosen, features, dims, preferred_element_type=jnp.float32) / snaps
    rhs = lax.dot_general(chosen, targets, dims, preferred_element_type=jnp.float32) / snaps
    return normal, rhs


def per_device(snapshots, basis):
    return row_block(all_states(snapshots, basis))


def solution(mesh):
    return jax.shard_map(
        per_device,
        mesh=mesh,
        in_specs=(P("space", "snap"), P("space", None)),
        out_specs=(P("snap", None), P("snap", None)),
        check_vma=False,
    )
```

time: 137 us -> 25.8 us (0.19)
  waiting for transfers between devices: 88.3 us -> 0 us
  Pallas kernels: 0 us -> 22.3 us
  between operations: 14.1 us -> 0.65 us
  local copies, waits for them, and re-layouts: 15.2 us -> 2.63 us
  matrix products: 8.58 us -> 0 us
  blocking collectives: 5.18 us -> 0 us
  other arithmetic: 4.27 us -> 0 us
    psum x1 -> x0, waiting for transfers between devices: 88.3 us -> none  [per_device(): summed = lax.psum(partial_value, 'space')]
    pallas_call x0 -> x2, Pallas kernels: none -> 22.3 us  [the longest x1 16.8 us: all_states(): pl.pallas_call(functools.partial(states_kernel, n, m), out_shape=jax.Shap...]
    gather x2 -> x0, local copies, waits for them, and re-layouts: 13.5 us -> none  [row_block(): quad = states[upper_rows, :] * states[upper_cols, :]]
    dot_general x3 -> x0, matrix products: 8.58 us -> none  [the longest x1 5.24 us: row_block(): lax.dot_general(chosen, features, dims, preferred_element_type=jnp.float32)]
    all_gather x1 -> x0, blocking collectives: 5.18 us -> none  [per_device(): states = lax.all_gather(summed, 'snap', axis=1, tiled=True)]
    another operation x2 -> x0, other arithmetic: 4.25 us -> none
  transfers between devices with their start and end apart: 1 -> 0, of which waited for: 1 -> 0; matrix products, arithmetic and copies ran while one was open for 0% -> 0% of each run, Pallas kernels for 0% -> 0%
where the time goes in v1:
time: 25.8 us; the launch traced here: 25.6 us
  Pallas kernels  22.3 us (86%)
  local copies, waits for them, and re-layouts  2.63 us (10%)
  between operations  0.65 us (3%)
    pallas_call x1, Pallas kernels, all_states(): pl.pallas_call(functools.partial(states_kernel, n, m), out_shape=jax.Shap...  16.8 us
    pallas_call x1, Pallas kernels, row_block(): pl.pallas_call(functools.partial(normal_kernel, m), out_shape=(jax.ShapeD...  5.54 us
    unnamed x4, local copies, waits for them, and re-layouts  2.63 us

profile of v1, /device:TPU:0, one launch (start us, length us, event | category | flops | bytes accessed | tf_op | source)
XLA Modules:
  0.0 25.6 jit_solution(13718580564243215621)
XLA Ops:
  0.6 0.0 copy-start
  0.6 1.6 %copy-done = bf16[4096,256]{1,0:T(8,128)(2,1)S(1)} copy-done((bf16[4096,256]{1,0:T(8,128)(2,1)S(1)}, bf16[4096,256]{1,0:T(8,128)(2,1)}, u32[]{:S(2)}) %copy-start) | copy-done | bytes 2097176
  2.2 0.0 copy-start.1
  2.2 1.0 %copy-done.1 = bf16[4096,64]{0,1:T(8,128)(2,1)S(1)} copy-done((bf16[4096,64]{0,1:T(8,128)(2,1)S(1)}, bf16[4096,64]{0,1:T(8,128)(2,1)}, u32[]{:S(2)}) %copy-start.1) | copy-done | bytes 524312
  3.3 16.8 %states.1.states_ref = f32[64,512]{1,0:T(8,128)S(1)} custom-call(bf16[4096,256]{1,0:T(8,128)(2,1)S(1)} %copy-done, bf16[64,4096]{1,0:T(8,128)(2,1)S(1)} %bitcast.2), custom_call_target="tpu_custom_call" | custom-call | tf_op jit(solution)/shard_map/states/pallas_call | solution.py:105
  20.0 5.5 %normal.1 = (f32[1072,2144]{1,0:T(8,128)}, f32[64,1072]{1,0:T(8,128)}) custom-call(f32[64,512]{1,0:T(8,128)S(1)} %states.1.states_ref), custom_call_target="tpu_custom_call" | custom-call | tf_op jit(solution)/shard_map/normal/pallas_call | solution.py:181
Async XLA Ops:
  0.6 1.6 %copy-start = (bf16[4096,256]{1,0:T(8,128)(2,1)S(1)}, bf16[4096,256]{1,0:T(8,128)(2,1)}, u32[]{:S(2)}) copy-start(bf16[4096,256]{1,0:T(8,128)(2,1)} %snaps_hbm.1) | copy-start | bytes 6291460
  2.2 1.0 %copy-start.1 = (bf16[4096,64]{0,1:T(8,128)(2,1)S(1)}, bf16[4096,64]{0,1:T(8,128)(2,1)}, u32[]{:S(2)}) copy-start(bf16[4096,64]{0,1:T(8,128)(2,1)} %param.3) | copy-start | bytes 1572868

commit v2 on v1

--- a/solution.py
+++ b/solution.py
@@ -11,11 +11,16 @@
 MESH = pl.DeviceIdType.MESH
 SUB, LANE = 8, 128
 LOADS = 4
+LIMIT = 107 * 2**19
+
+
+def far_first(n):
+    return sorted(range(1, n), key=lambda d: (-min(d, n - d), d))
 
 
 def states_kernel(n, m, snaps_hbm, basis_hbm, out_ref, snaps, basis, part, recv, gath, load_sem, sems):
     me, grp = lax.axis_index("space"), lax.axis_index("snap")
-    peers = [(dp, ds) for ds in range(m) for dp in range(n) if dp or ds]
+    peers = [(dp, ds) for ds in range(m) for dp in far_first(n) + [0] if dp or ds]
 
     step = snaps.shape[0] // LOADS
     loads = []
@@ -55,7 +60,7 @@
 
     pl.semaphore_wait(barrier, len(peers))
 
-    for dp in range(1, n):
+    for dp in far_first(n):
         to = device(dp, 0)
         pltpu.make_async_remote_copy(
             src_ref=part.at[to[0]],
@@ -105,7 +110,7 @@
     return pl.pallas_call(
         functools.partial(states_kernel, n, m),
         out_shape=jax.ShapeDtypeStruct((rank, width * m), jnp.float32),
-        in_specs=[pl.BlockSpec(memory_space=pl.ANY)] * 2,
+        in_specs=[pl.BlockSpec(memory_space=pltpu.HBM)] * 2,
         out_specs=pl.BlockSpec(memory_space=pltpu.VMEM),
         scratch_shapes=[
             pltpu.VMEM((rows, width), jnp.bfloat16),
@@ -117,7 +122,7 @@
             pltpu.SemaphoreType.DMA((4,)),
         ],
         compiler_params=pltpu.CompilerParams(
-            collective_id=0, has_side_effects=True, vmem_limit_bytes=32 * 2**20
+            collective_id=0, has_side_effects=True, vmem_limit_bytes=LIMIT
         ),
         name="states",
     )(snapshots, basis.T)

time: 25.8 us -> 23.5 us (0.911)
  local copies, waits for them, and re-layouts: 2.63 us -> 0 us
  Pallas kernels: 22.3 us -> 22.7 us
    unnamed x4 -> x0, local copies, waits for them, and re-layouts: 2.63 us -> none
    pallas_call x1, Pallas kernels: 16.8 us -> 17.1 us  [all_states(): pl.pallas_call(functools.partial(states_kernel, n, m), out_shape=jax.Shap...]
where the time goes in v2:
time: 23.5 us; the launch traced here: 23.3 us
  Pallas kernels  22.7 us (97%)
  between operations  0.64 us (3%)
    pallas_call x1, Pallas kernels, all_states(): pl.pallas_call(functools.partial(states_kernel, n, m), out_shape=jax.Shap...  17.1 us
    pallas_call x1, Pallas kernels, row_block(): pl.pallas_call(functools.partial(normal_kernel, m), out_shape=(jax.ShapeD...  5.54 us

profile of v2, /device:TPU:0, one launch (start us, length us, event | category | flops | bytes accessed | tf_op | source)
XLA Modules:
  0.0 23.3 jit_solution(6144717364009155071)
XLA Ops:
  0.6 17.1 %states.1.states_ref = f32[64,512]{1,0:T(8,128)S(1)} custom-call(bf16[4096,256]{1,0:T(8,128)(2,1)} %snaps_hbm.1, bf16[64,4096]{1,0:T(8,128)(2,1)} %bitcast.2), custom_call_target="tpu_custom_call" | custom-call | tf_op jit(solution)/shard_map/states/pallas_call | solution.py:110
  17.8 5.5 %normal.1 = (f32[1072,2144]{1,0:T(8,128)}, f32[64,1072]{1,0:T(8,128)}) custom-call(f32[64,512]{1,0:T(8,128)S(1)} %states.1.states_ref), custom_call_target="tpu_custom_call" | custom-call | tf_op jit(solution)/shard_map/normal/pallas_call | solution.py:186
